TPU v7x, 32 devices: a whole 2x2x4 slice. The times are simulated.
32 devices in a mesh: group: 2 (over x), expert: 16 (over z, y, core), tensor: 1.
Axes of the slice: x: 2, y: 2, z: 4, core: 2. Of those that a mesh axis runs over, the one named last changes fastest.
Arguments:
- tokens: bfloat16 [4096, 3584], P(('group', 'expert'), 'tensor'), parts along dimension 0, may hold values from -6 to 6
- routes: int32 [4096, 8], P(('group', 'expert')), parts along dimension 0, may hold values from 0 to 16, all different within a row; in each aligned block of 128 rows (0 to 127, 128 to 255, ...) at most 64 rows name the same one
- gate_q: int32 [4096, 8], P(('group', 'expert')), parts along dimension 0, may hold values from 1 to 255
- hot_list: int32 [1], replicated, may hold values from 0 to 16
- cold_gate_up: bfloat16 [16, 2, 3584, 1024], P('expert', None, None, 'tensor'), may hold values from -0.09375 to 0.09375
- cold_down: bfloat16 [16, 1024, 3584], P('expert', 'tensor'), may hold values from -0.1875 to 0.1875
- hot_gate_up: bfloat16 [1, 2, 3584, 1024], P(None, None, None, 'tensor'), may hold values from -0.09375 to 0.09375
- hot_down: bfloat16 [1, 1024, 3584], P(None, 'tensor'), may hold values from -0.1875 to 0.1875
Outputs:
- mixed: bfloat16 [4096, 3584], P(('group', 'expert'), 'tensor'), parts along dimension 0
There are 2 independent parts, one for each index of `group`. A program takes and returns all parts, laid end to end along the dimension named above; an argument that names none is the same for every part. Nothing has to cross between parts.
Inputs may be any that keep to these rules, and one draw needn't show every extreme that they name: `routes`: each row names 8 distinct experts; within the 128 rows of one index of expert, no expert is named by more than 64 rows, a bound that some block reaches. `hot_list`: the hot ids are distinct.
All inputs are finite; a program needn't handle non-finite values.
Results may differ from a plain program's by a relative error of at most 0.0065.
Values may be sent and summed in bfloat16 or wider, within the bound.
A program may use at most 128 MiB of HBM per device.

v0:
```python
import jax
import jax.numpy as jnp
from jax import lax
from jax.sharding import PartitionSpec as P

TOP = 8
HOT = 1


def slot_table(hot_list, experts_all):
    labels = jnp.arange(experts_all, dtype=jnp.int32)
    hot_match = (hot_list[:, None] == labels[None, :]).astype(jnp.int32)
    is_hot = jnp.sum(hot_match, axis=0)
    cold_rank = jnp.cumsum(1 - is_hot) - 1
    return (is_hot, cold_rank, hot_match)


def route_weights(routes, gate_q, experts_all):
    quantized = gate_q.astype(jnp.float32)
    shares = quantized / jnp.sum(quantized, axis=1, keepdims=True)
    labels = jnp.arange(experts_all, dtype=jnp.int32)
    picked = routes[:, :, None] == labels[None, None, :]
    chosen = jnp.sum(picked.astype(jnp.int32), axis=1)
    weight = jnp.sum(jnp.where(picked, shares[:, :, None], jnp.float32(0.0)), axis=1)
    return (chosen, weight, shares)


def swiglu(inputs, gate_up, down_proj):
    paired = jnp.einsum("snd,gdf->gsnf", inputs, gate_up, preferred_element_type=jnp.float32)
    hidden = (jax.nn.silu(paired[0]) * paired[1]).astype(jnp.bfloat16)
    return jnp.einsum("snf,fd->snd", hidden, down_proj, preferred_element_type=jnp.float32)


def local(tokens, routes, gate_q, hot_list, cold_gate_up, cold_down, hot_gate_up, hot_down):
    experts_cold = lax.axis_size("expert")
    experts_all = experts_cold + HOT
    local_rows = tokens.shape[0]
    capacity = local_rows * TOP // experts_cold
    is_hot, cold_rank, hot_match = slot_table(hot_list, experts_all)
    chosen, weight, shares = route_weights(routes, gate_q, experts_all)
    placed = jnp.cumsum(chosen, axis=0) - 1
    slot_hit = (
        (placed[:, :, None] == jnp.arange(capacity, dtype=jnp.int32)[None, None, :])
        & (chosen[:, :, None] > 0)
    ).astype(jnp.bfloat16)
    target = (
        (cold_rank[None, :] == jnp.arange(experts_cold, dtype=jnp.int32)[:, None])
        & (is_hot[None, :] == 0)
    ).astype(jnp.bfloat16)
    scatter_plan = jnp.einsum(
        "de,rec->dcr", target, slot_hit, preferred_element_type=jnp.float32
    ).astype(jnp.bfloat16)
    outgoing = jnp.einsum(
        "dcr,rk->dck", scatter_plan, tokens, preferred_element_type=jnp.float32
    ).astype(jnp.bfloat16)
    route_hot = jnp.take(is_hot, routes, axis=0)
    route_rank = jnp.take(cold_rank, routes, axis=0)
    route_place = jnp.take_along_axis(placed, routes, axis=1)
    flat_index = jnp.where(route_hot > 0, 0, route_rank * capacity + route_place)
    cold_share = jnp.where(route_hot > 0, jnp.float32(0.0), shares)
    hot_weight = jnp.sum(weight[:, None, :] * hot_match[None, :, :].astype(jnp.float32), axis=2)
    hot_paired = jnp.einsum(
        "rn,hgnf->hgrf",
        lax.all_gather(tokens, "tensor", axis=1, tiled=True),
        hot_gate_up,
        preferred_element_type=jnp.float32,
    )
    hot_hidden = (jax.nn.silu(hot_paired[:, 0]) * hot_paired[:, 1]).astype(jnp.bfloat16)
    hot_part = jnp.einsum("hrf,hfd->hrd", hot_hidden, hot_down, preferred_element_type=jnp.float32)
    hot_answer = lax.psum_scatter(
        hot_part.astype(jnp.bfloat16), "tensor", scatter_dimension=2, tiled=True
    )
    hot_total = jnp.sum(
        jnp.transpose(hot_weight)[:, :, None] * hot_answer.astype(jnp.float32), axis=0
    )
    widened = lax.all_gather(
        lax.all_to_all(outgoing, "expert", split_axis=0, concat_axis=0, tiled=True),
        "tensor",
        axis=2,
        tiled=True,
    )
    partial_out = swiglu(widened, cold_gate_up[0], cold_down[0])
    answers = lax.psum_scatter(partial_out, "tensor", scatter_dimension=2, tiled=True).astype(
        jnp.bfloat16
    )
    returned = lax.all_to_all(answers, "expert", split_axis=0, concat_axis=0, tiled=True)
    feature_part = returned.shape[2]
    flat_answers = returned.reshape(experts_cold * capacity, feature_part)
    picked_rows = jnp.take(flat_answers, flat_index.reshape(-1), axis=0).reshape(
        local_rows, TOP, feature_part
    )
    cold_total = jnp.sum(cold_share[:, :, None] * picked_rows.astype(jnp.float32), axis=1)
    return (cold_total + hot_total).astype(jnp.bfloat16)


def solution(mesh):
    return jax.shard_map(
        local,
        mesh=mesh,
        in_specs=(
            P(("group", "expert"), "tensor"),
            P(("group", "expert"), None),
            P(("group", "expert"), None),
            P(),
            P("expert", None, None, "tensor"),
            P("expert", "tensor", None),
            P(None, None, None, "tensor"),
            P(None, "tensor", None),
        ),
        out_specs=P(("group", "expert"), "tensor"),
        check_vma=False,
    )
```

profile of v0, /device:TPU:13, one launch (start us, length us, event | category | flops | bytes accessed | tf_op | source)
XLA Modules:
  0.0 406.9 jit_solution(12103888106586570300)
XLA Ops:
  0.0 0.8 convert_reduce_fusion
  0.8 0.1 copy.58
  1.6 0.1 add_reduce_fusion
  1.7 0.2 reduce_window_sum.18
  1.9 0.1 copy.62
  2.1 1.7 fusion.40
  3.8 2.1 convolution_convert_fusion
  5.9 0.0 slice-start
  5.9 166.3 %all_to_all.10 = bf16[16,64,3584]{2,1,0:T(8,128)(2,1)S(1)} all-to-all(bf16[16,64,3584]{2,1,0:T(8,128)(2,1)S(1)} %convolution_convert_fusion), channel_id=1, replica_groups=mesh['group'=2,'expert'=16,'tensor'=1] {'expert'}, dimensions={0} | all-to-all | bytes 14680064 | tf_op jit(solution)/shard_map/all_to_all | solution.py:77
  172.2 19.4 %fusion.24 = f32[2,16,64,1024]{3,2,0,1:T(8,128)} fusion(bf16[1,2,3584,1024]{3,2,1,0:T(8,128)(2,1)} %param.14, bf16[16,64,3584]{2,1,0:T(8,128)(2,1)S(1)} %all_to_all.10), kind=kOutput, calls=%fused_computation.21 | convolution fusion | flops 15032385536 | bytes 30408704 | tf_op jit(solution)/shard_map/snd,gdf->gsnf/dot_general | solution.py:29
  191.5 0.0 slice-done.1
  191.5 14.5 %convolution_convert_fusion.1 = bf16[16,64,3584]{2,1,0:T(8,128)(2,1)} fusion(bf16[1,1024,3584]{2,1,0:T(8,128)(2,1)S(1)} %bitcast.107, f32[2,16,64,1024]{3,2,0,1:T(8,128)} %fusion.24), kind=kOutput, calls=%fused_computation.8 | convolution fusion | flops 7526154240 | bytes 23068672 | tf_op jit(solution)/shard_map/snf,fd->snd/dot_general | solution.py:31
  206.0 5.8 %all-to-all-start.1 = ((bf16[16,64,3584]{2,1,0:T(8,128)(2,1)}), bf16[16,64,3584]{2,1,0:T(8,128)(2,1)}, u32[]{:S(2)}, u32[]{:S(2)}) async-start(bf16[16,64,3584]{2,1,0:T(8,128)(2,1)} %convolution_convert_fusion.1), calls=%async_computation.1 | async-start | bytes 14680064 | tf_op jit(solution)/shard_map/all_to_all | solution.py:86
  211.8 0.1 copy.59
  211.9 0.1 reshape.235
  212.0 0.0 copy-start.2
  212.0 7.1 %gather_fusion.1 = s32[1024]{0:T(1024)S(1)} fusion(s32[128,17]{1,0:T(8,128)S(1)} %broadcast_add_fusion, s32[1024]{0:T(1024)S(1)} %reshape.235), kind=kCustom, calls=%fused_computation.1 | custom fusion | bytes 16384 | tf_op jit(solution)/shard_map/jit(take_along_axis)/gather | solution.py:58
  219.1 0.1 reshape.238
  219.2 0.7 fusion.63
  220.0 0.7 fusion.62
  220.7 21.4 %compare_and_fusion.1 = (pred[128,8]{0,1:T(8,128)(4,1)S(1)}, s32[128,8]{0,1:T(8,128)S(1)}, pred[128,8]{0,1:T(8,128)(4,1)S(1)}) fusion(pred[128,8]{0,1:T(8,128)(4,1)S(1)} %get-tuple-element.12, s32[128,8]{0,1:T(8,128)S(1)} %copy.60, pred[128,8]{0,1:T(8,128)(4,1)S(1)} %get-tuple-element.13, pred[128,8]{0,1:T(8,128)(4,1)S(1)} %get-tuple-element.14, ...), kind=kLoop, calls=%fused_computation.62 | loop fusion | flops 46080 | bytes 27784 | tf_op jit(solution)/shard_map/jit(_take)/and | solution.py:89
  242.1 0.1 copy.64
  242.2 0.1 reshape.176
  242.3 0.0 copy-done.2
  242.3 0.1 copy.57
  242.4 0.1 copy.61
  242.6 0.1 multiply_reduce_fusion.1
  242.7 7.4 %fusion.34 = f32[1,2,128,1024]{2,3,1,0:T(8,128)S(1)} fusion(bf16[1,2,3584,1024]{3,2,1,0:T(8,128)(2,1)} %param.16, bf16[128,3584]{1,0:T(8,128)(2,1)S(1)} %copy-done), kind=kOutput, calls=%fused_computation.26 | convolution fusion | flops 1879048192 | bytes 16646144 | tf_op jit(solution)/shard_map/rn,hgnf->hgrf/dot_general | solution.py:62
  250.2 121.5 %all-to-all-done.1 = bf16[16,64,3584]{2,1,0:T(8,128)(2,1)} async-done(((bf16[16,64,3584]{2,1,0:T(8,128)(2,1)}), bf16[16,64,3584]{2,1,0:T(8,128)(2,1)}, u32[]{:S(2)}, u32[]{:S(2)}) %all-to-all-start.1) | async-done | bytes 7340064 | tf_op jit(solution)/shard_map/all_to_all | solution.py:86
  371.6 17.8 %gather_fusion = bf16[1024,3584]{1,0:T(8,128)(2,1)} fusion(bf16[1024,3584]{1,0:T(8,128)(2,1)} %bitcast.47, s32[1024]{0:T(1024)S(1)} %broadcast_clamp_fusion), kind=kCustom, calls=%fused_computation | custom fusion | bytes 14684160 | tf_op jit(solution)/shard_map/jit(_take)/gather | solution.py:89
  389.4 12.1 %multiply_reduce_fusion = f32[128,3584]{1,0:T(8,128)S(1)} fusion(bf16[1024,3584]{1,0:T(8,128)(2,1)} %gather_fusion, f32[128,8]{1,0:T(8,128)S(1)} %copy.57, pred[128,8]{1,0:T(8,128)(4,1)S(1)} %copy.61), kind=kLoop, calls=%fused_computation.6 | loop fusion | flops 14221312 | bytes 9180160 | tf_op jit(solution)/shard_map/reduce_sum | solution.py:92
  401.5 5.3 %fusion.20 = bf16[128,3584]{1,0:T(8,128)(2,1)} fusion(f32[128,3584]{1,0:T(8,128)S(1)} %multiply_reduce_fusion, bf16[1,1024,3584]{2,1,0:T(8,128)(2,1)} %param.17, f32[128]{0:T(128)S(1)} %multiply_reduce_fusion.1, f32[1,2,128,1024]{2,3,1,0:T(8,128)S(1)} %fusion.34), kind=kOutput, calls=%fused_computation.18 | convolution fusion | flops 942604288 | bytes 11141632 | tf_op jit(solution)/shard_map/hrf,hfd->hrd/dot_general | solution.py:69
  (21 shorter events, 0.2 us)
Async XLA Ops:
  0.0 3.8 copy-start
  5.9 185.7 %slice-start = ((s8[7340032]{0:T(1024)(128)(4,1)}), s8[4194304]{0:T(1024)(128)(4,1)S(1)}, s32[]{:S(2)}) async-start(s8[7340032]{0:T(1024)(128)(4,1)} %bitcast.106), calls=%async_computation.2 | async-start | bytes 8388608
  172.2 19.4 %slice-start.1 = ((s8[7340032]{0:T(1024)(128)(4,1)}), s8[3145728]{0:T(1024)(128)(4,1)S(1)}, s32[]{:S(2)}) async-start(s8[7340032]{0:T(1024)(128)(4,1)} %bitcast.106), calls=%async_computation.3 | async-start | bytes 6291456
  206.0 5.8 %copy-start.1 = (s32[128,8]{0,1:T(8,128)S(1)}, s32[128,8]{0,1:T(8,128)}, u32[]{:S(2)}) copy-start(s32[128,8]{0,1:T(8,128)} %param.11) | copy-start | bytes 12292
  206.0 165.6 %all-to-all-start.1 = ((bf16[16,64,3584]{2,1,0:T(8,128)(2,1)}), bf16[16,64,3584]{2,1,0:T(8,128)(2,1)}, u32[]{:S(2)}, u32[]{:S(2)}) async-start(bf16[16,64,3584]{2,1,0:T(8,128)(2,1)} %convolution_convert_fusion.1), calls=%async_computation.1 | async-start | bytes 14680064 | tf_op jit(solution)/shard_map/all_to_all | solution.py:86
  212.0 30.3 %copy-start.2 = (s32[128,8]{0,1:T(8,128)S(1)}, s32[128,8]{0,1:T(8,128)}, u32[]{:S(2)}) copy-start(s32[128,8]{0,1:T(8,128)} %param.12) | copy-start | bytes 12292
where the time goes:
time: 408 us; the launch traced here: 407 us
  blocking collectives  166 us (41%)
  waiting for transfers between devices  121 us (30%)
  matrix products  50.4 us (12%)
  other arithmetic  34.8 us (9%)
  local copies, waits for them, and re-layouts  27.3 us (7%)
  starting transfers between devices  5.76 us (1%)
    all_to_all x1, blocking collectives, local(): lax.all_to_all(outgoing, 'expert', split_axis=0, concat_axis=0, tiled=True)  166 us
    all_to_all x1, waiting for transfers between devices, local(): lax.all_to_all(answers, 'expert', split_axis=0, concat_axis=0, tiled=True)  121 us
    and x1, other arithmetic, local(): jnp.take(flat_answers, flat_index.reshape(-1), axis=0)  21.4 us
    dot_general x1, matrix products, swiglu(): jnp.einsum('snd,gdf->gsnf', inputs, gate_up, preferred_element_type=jnp.f...  19.4 us
    gather x1, local copies, waits for them, and re-layouts, local(): jnp.take(flat_answers, flat_index.reshape(-1), axis=0)  17.8 us
    dot_general x1, matrix products, swiglu(): jnp.einsum('snf,fd->snd', hidden, down_proj, preferred_element_type=jnp.f...  14.5 us
    reduce_sum x1, other arithmetic, local(): jnp.sum(cold_share[:, :, None] * picked_rows.astype(jnp.float32), axis=1)  12.1 us
  transfers between devices with their start and end apart: 1, of which 1 were waited for; matrix products, arithmetic and copies ran while one was open for 9% of the time, Pallas kernels for 0%

commit v1 on v0

--- a/solution.py
+++ b/solution.py
@@ -1,10 +1,402 @@
+import functools
+
 import jax
 import jax.numpy as jnp
 from jax import lax
+from jax.experimental import pallas as pl
+from jax.experimental.pallas import tpu as pltpu
 from jax.sharding import PartitionSpec as P
 
 TOP = 8
 HOT = 1
+NZ, NY, NC = 4, 2, 2
+LANES = 128
+F32 = jnp.float32
+BF16 = jnp.bfloat16
+
+
+def place():
+    e = lax.axis_index("expert")
+    return e // (NY * NC), (e // NC) % NY, e % NC
+
+
+def index(z, y, c):
+    return (z * NY + y) * NC + c
+
+
+def greet(z, y, c):
+    barrier = pltpu.get_barrier_semaphore()
+
+    def hello(dev):
+        pl.semaphore_signal(
+            barrier, inc=1, device_id={"expert": dev}, device_id_type=pl.DeviceIdType.MESH
+        )
+
+    hello(index(z, y, 1 - c))
+    hello(index(z, 1 - y, c))
+
+    @pl.when(z > 0)
+    def _():
+        hello(index(z - 1, y, c))
+
+    @pl.when(z < NZ - 1)
+    def _():
+        hello(index(z + 1, y, c))
+
+    ends = (z == 0) | (z == NZ - 1)
+
+    @pl.when(ends)
+    def _():
+        pl.semaphore_wait(barrier, 3)
+
+    @pl.when(jnp.logical_not(ends))
+    def _():
+        pl.semaphore_wait(barrier, 4)
+
+
+def spread_kernel(first, x_ref, out_ref, own_sem, send_sem, recv_sem):
+    z, y, c = place()
+    rows = x_ref.shape[0]
+    parts = (pl.ds(0, first), pl.ds(first, rows - first))
+    up, down, side, core = 0, 1, 2, 3
+    own = index(z, y, c)
+    keep = pltpu.make_async_copy(x_ref, out_ref.at[own], own_sem)
+    keep.start()
+    greet(z, y, c)
+
+    def copy(way, source, part, from_input=False):
+        target = (index(z + 1, y, c), index(z - 1, y, c), index(z, 1 - y, c), index(z, y, 1 - c))[way]
+        block = x_ref if from_input else out_ref.at[source]
+        return pltpu.make_async_remote_copy(
+            src_ref=block.at[parts[part]],
+            dst_ref=out_ref.at[source, parts[part]],
+            send_sem=send_sem.at[way, source, part],
+            recv_sem=recv_sem.at[source, part],
+            device_id={"expert": target},
+            device_id_type=pl.DeviceIdType.MESH,
+        )
+
+    def send(way, source, part, go=None, from_input=False):
+        if go is None:
+            copy(way, source, part, from_input).start()
+        else:
+            pl.when(go)(lambda: copy(way, source, part, from_input).start())
+
+    def arrived(source, part):
+        copy(core, source, part).wait_recv()
+
+    def sent(way, source, part, go=None):
+        if go is None:
+            copy(way, source, part).wait_send()
+        else:
+            pl.when(go)(lambda: copy(way, source, part).wait_send())
+
+    has_up, has_down = z < NZ - 1, z > 0
+    beside = index(z, 1 - y, c)
+    for part in (1, 0):
+        send(up, own, part, has_up, True)
+        send(down, own, part, has_down, True)
+        send(side, own, part, None, True)
+    for part in (0, 1):
+        send(core, own, part, None, True)
+    arrived(beside, 1)
+    send(up, beside, 1, has_up)
+    send(down, beside, 1, has_down)
+    send(core, beside, 1)
+
+    def step(k, finish):
+        for way in (up, down):
+            zs = z - k if way == up else z + k
+            there = (zs >= 0) if way == up else (zs < NZ)
+            onward = has_up if way == up else has_down
+
+            @pl.when(there)
+            def _():
+                mine, other = index(zs, y, c), index(zs, 1 - y, c)
+                order = ((mine, 1), (mine, 0), (other, 1))
+                for source, part in order:
+                    if finish:
+                        sent(way, source, part, onward)
+                        sent(core, source, part)
+                    else:
+                        arrived(source, part)
+                        send(way, source, part, onward)
+                        if part == 0:
+                            send(side, source, part)
+                        send(core, source, part)
+                if finish:
+                    sent(side, mine, 0)
+
+    def cross(k, finish):
+        for zs, there in ((z - k, z - k >= 0), (z + k, z + k < NZ)):
+
+            @pl.when(there)
+            def _():
+                other = index(zs, 1 - y, c)
+                if finish:
+                    sent(core, other, 0)
+                else:
+                    arrived(other, 0)
+                    send(core, other, 0)
+
+    for k in range(1, NZ):
+        step(k, False)
+        if k == 1:
+            arrived(beside, 0)
+            send(core, beside, 0)
+        else:
+            cross(k - 1, False)
+    cross(NZ - 1, False)
+    for zs in range(NZ):
+        for ys in range(NY):
+            for part in (0, 1):
+                arrived(index(zs, ys, 1 - c), part)
+    for part in (1, 0):
+        sent(up, own, part, has_up)
+        sent(down, own, part, has_down)
+        sent(side, own, part)
+        sent(core, own, part)
+        sent(core, beside, part)
+    sent(up, beside, 1, has_up)
+    sent(down, beside, 1, has_down)
+    for k in range(1, NZ):
+        step(k, True)
+        cross(k, True)
+    keep.wait()
+
+
+def spread(x, first):
+    n = NZ * NY * NC
+    return pl.pallas_call(
+        functools.partial(spread_kernel, first),
+        out_shape=jax.ShapeDtypeStruct((n,) + x.shape, x.dtype),
+        in_specs=[pl.BlockSpec(memory_space=pl.ANY)],
+        out_specs=pl.BlockSpec(memory_space=pl.ANY),
+        scratch_shapes=[
+            pltpu.SemaphoreType.DMA,
+            pltpu.SemaphoreType.DMA((4, n, 2)),
+            pltpu.SemaphoreType.DMA((n, 2)),
+        ],
+        compiler_params=pltpu.CompilerParams(collective_id=0, has_side_effects=True),
+    )(x)
+
+
+def fold_kernel(
+    first, p_ref, hot_ref, o_ref, core_in, side_a, side_b, line_a, line_b, out_ya, out_yb, out_za, out_zb,
+    core_s, core_r, ya_s, ya_r, yb_s, yb_r, za_s, za_r, zb_s, zb_r,
+):
+    z, y, c = place()
+    rows = o_ref.shape[0]
+    part_a, part_b = (0, first), (first, rows - first)
+    greet(z, y, c)
+
+    def remote(src, dst, s, r, target):
+        return pltpu.make_async_remote_copy(
+            src_ref=src, dst_ref=dst, send_sem=s, recv_sem=r,
+            device_id={"expert": target}, device_id_type=pl.DeviceIdType.MESH,
+        )
+
+    def core_copy(zd, yd):
+        return remote(p_ref.at[index(zd, yd, 1 - c)], core_in.at[zd, yd], core_s.at[zd, yd], core_r.at[zd, yd], index(z, y, 1 - c))
+
+    def ya_copy(zd):
+        return remote(out_ya.at[zd], side_a.at[zd], ya_s.at[zd], ya_r.at[zd], index(z, 1 - y, c))
+
+    def yb_copy():
+        return remote(out_yb, side_b, yb_s, yb_r, index(z, 1 - y, c))
+
+    def za_copy(way, zd):
+        return remote(out_za.at[zd], line_a.at[way, zd], za_s.at[zd], za_r.at[way, zd], index(z + 1 - 2 * way, y, c))
+
+    def zb_copy(way, zd, yd):
+        return remote(out_zb.at[zd, yd], line_b.at[way, zd, yd], zb_s.at[zd, yd], zb_r.at[way, zd, yd], index(z + 1 - 2 * way, y, c))
+
+    def add(dst, part, *sources):
+        def one(i, carry):
+            at = pl.multiple_of(i * 16, 16)
+            total = sources[0][0][pl.ds(sources[0][1] + at, 16), :].astype(F32)
+            for ref, start in sources[1:]:
+                total = total + ref[pl.ds(start + at, 16), :].astype(F32)
+            dst[0][pl.ds(dst[1] + at, 16), :] = total.astype(dst[0].dtype)
+            return carry
+
+        lax.fori_loop(0, part[1] // 16, one, 0)
+
+    def each(k, f):
+        if k == 0:
+            f(z, None)
+        else:
+            pl.when(z + k < NZ)(lambda: f(z + k, 0))
+            pl.when(z - k >= 0)(lambda: f(z - k, 1))
+
+    def start_core(zd, way):
+        for yd in range(NY):
+            core_copy(zd, yd).start()
+
+    def over_core(zd, way):
+        core_copy(zd, 1 - y).wait_recv()
+        add((out_ya.at[zd], 0), part_a, (p_ref.at[index(zd, 1 - y, c)], 0), (core_in.at[zd, 1 - y], 0))
+        ya_copy(zd).start()
+        core_copy(zd, y).wait_recv()
+
+    def along(zd, way):
+        first_of_line = (z == 0) if way == 0 else (z == NZ - 1)
+
+        for yd in range(NY):
+            base = ((p_ref.at[index(zd, yd, c)], first), (core_in.at[zd, yd], first))
+
+            @pl.when(first_of_line)
+            def _():
+                add((out_zb.at[zd, yd], 0), part_b, *base)
+
+            @pl.when(jnp.logical_not(first_of_line))
+            def _():
+                zb_copy(way, zd, yd).wait_recv()
+                add((out_zb.at[zd, yd], 0), part_b, *base, (line_b.at[way, zd, yd], 0))
+
+            zb_copy(way, zd, yd).start()
+        ya_copy(zd).wait_recv()
+        base = ((p_ref.at[index(zd, y, c)], 0), (core_in.at[zd, y], 0), (side_a.at[zd], 0))
+
+        @pl.when(first_of_line)
+        def _():
+            add((out_za.at[zd], 0), part_a, *base)
+
+        @pl.when(jnp.logical_not(first_of_line))
+        def _():
+            za_copy(way, zd).wait_recv()
+            add((out_za.at[zd], 0), part_a, *base, (line_a.at[way, zd], 0))
+
+        za_copy(way, zd).start()
+
+    def finish(zd):
+        def by_end(f):
+            pl.when(z == 0)(lambda: f((1,)))
+            pl.when(z == NZ - 1)(lambda: f((0,)))
+            pl.when((z > 0) & (z < NZ - 1))(lambda: f((0, 1)))
+
+        def last_b(ways):
+            for yd, dst in ((1 - y, out_yb), (y, None)):
+                for way in ways:
+                    zb_copy(way, zd, yd).wait_recv()
+                base = ((p_ref.at[index(zd, yd, c)], first), (core_in.at[zd, yd], first)) + tuple(
+                    (line_b.at[way, zd, yd], 0) for way in ways
+                )
+                if dst is None:
+                    yb_copy().wait_recv()
+                    add((o_ref, first), part_b, *base, (side_b, 0), (hot_ref, first))
+                else:
+                    add((dst, 0), part_b, *base)
+                    yb_copy().start()
+
+        def last_a(ways):
+            for way in ways:
+                za_copy(way, zd).wait_recv()
+            add(
+                (o_ref, 0), part_a, (p_ref.at[index(zd, y, c)], 0), (core_in.at[zd, y], 0), (side_a.at[zd], 0),
+                (hot_ref, 0), *((line_a.at[way, zd], 0) for way in ways),
+            )
+
+        ya_copy(zd).wait_recv()
+        by_end(last_b)
+        by_end(last_a)
+
+    def drain(zd, way):
+        for yd in range(NY):
+            core_copy(zd, yd).wait_send()
+        ya_copy(zd).wait_send()
+        if way is None:
+            yb_copy().wait_send()
+        else:
+            za_copy(way, zd).wait_send()
+            for yd in range(NY):
+                zb_copy(way, zd, yd).wait_send()
+
+    for k in (3, 2, 1, 0):
+        each(k, start_core)
+    each(3, over_core)
+    each(2, over_core)
+    each(3, along)
+    each(1, over_core)
+    each(2, along)
+    each(0, over_core)
+    each(1, along)
+    finish(z)
+    for k in (3, 2, 1, 0):
+        each(k, drain)
+
+
+def fold(parts, hot, first):
+    n, rows, width = parts.shape
+    rest = rows - first
+    dma = pltpu.SemaphoreType.DMA
+    return pl.pallas_call(
+        functools.partial(fold_kernel, first),
+        out_shape=jax.ShapeDtypeStruct((rows, width), BF16),
+        in_specs=[pl.BlockSpec(memory_space=pltpu.VMEM)] * 2,
+        out_specs=pl.BlockSpec(memory_space=pltpu.VMEM),
+        scratch_shapes=[
+            pltpu.VMEM((NZ, NY, rows, width), BF16),
+            pltpu.VMEM((NZ, first, width), BF16),
+            pltpu.VMEM((rest, width), BF16),
+            pltpu.VMEM((2, NZ, first, width), BF16),
+            pltpu.VMEM((2, NZ, NY, rest, width), BF16),
+            pltpu.VMEM((NZ, first, width), BF16),
+            pltpu.VMEM((rest, width), BF16),
+            pltpu.VMEM((NZ, first, width), BF16),
+            pltpu.VMEM((NZ, NY, rest, width), BF16),
+            dma((NZ, NY)), dma((NZ, NY)),
+            dma((NZ,)), dma((NZ,)),
+            dma, dma,
+            dma((NZ,)), dma((2, NZ)),
+            dma((NZ, NY)), dma((2, NZ, NY)),
+        ],
+        compiler_params=pltpu.CompilerParams(
+            collective_id=1, has_side_effects=True, vmem_limit_bytes=60 * 2**20
+        ),
+    )(parts, hot)
+
+
+def meshed(tokens, routes, gate_q, hot_list, cold_gate_up, cold_down, hot_gate_up, hot_down):
+    n = lax.axis_size("expert")
+    rows, width = tokens.shape
+    capacity = rows * TOP // n
+    first = rows - 16
+    is_hot, cold_rank, hot_match = slot_table(hot_list, n + HOT)
+    picked = routes[:, :, None] == jnp.arange(n + HOT, dtype=jnp.int32)[None, None, :]
+    by_label = jnp.sum(jnp.where(picked, gate_q[:, :, None], 0), axis=1)
+    to_slot = jnp.where(is_hot > 0, n, cold_rank)
+    slot_of = to_slot[:, None] == jnp.arange(n + 1, dtype=jnp.int32)[None, :]
+    by_slot = jnp.sum(jnp.where(slot_of[None], by_label[:, :, None], 0), axis=1)
+    whole = jnp.sum(gate_q, axis=1, keepdims=True)
+    extra = jnp.concatenate([by_slot[:, :n], whole // 256, whole % 256], axis=1).astype(BF16)
+    extra = jnp.pad(extra, ((0, 0), (0, LANES - extra.shape[1])))
+    everything = spread(jnp.concatenate([tokens, extra], axis=1), first)
+
+    notes = everything[:, :, width:].astype(F32)
+    slot = lax.axis_index("expert")
+    gate = jnp.sum(jnp.where(jnp.arange(LANES) == slot, notes, 0.0), axis=2)
+    total = notes[:, :, n] * 256.0 + notes[:, :, n + 1]
+    share = gate / total
+    taken = gate > 0
+    rank = jnp.cumsum(taken.astype(jnp.int32), axis=1) - 1
+    hit = (rank[:, :, None] == jnp.arange(capacity, dtype=jnp.int32)) & taken[:, :, None]
+    hit = hit.astype(BF16)
+    x = jnp.einsum("brc,brd->bcd", hit, everything[:, :, :width], preferred_element_type=F32)
+    x = x.astype(BF16).reshape(n * capacity, width)
+    answers = expert(x, cold_gate_up[0], cold_down[0]).reshape(n, capacity, width)
+    part = jnp.einsum("brc,bcd->brd", hit, answers, preferred_element_type=F32)
+    part = (part * share[:, :, None]).astype(BF16)
+
+    hot_share = by_slot[:, n:].astype(F32) / whole.astype(F32)
+    hot = hot_share * expert(tokens, hot_gate_up[0], hot_down[0]).astype(F32)
+    return fold(part, hot, first)
+
+
+def expert(x, gate_up, down):
+    paired = jnp.einsum("nd,gdf->gnf", x, gate_up, preferred_element_type=F32)
+    hidden = (jax.nn.silu(paired[0]) * paired[1]).astype(BF16)
+    return jnp.einsum("nf,fd->nd", hidden, down, preferred_element_type=F32).astype(BF16)
 
 
 def slot_table(hot_list, experts_all):
@@ -94,8 +486,9 @@
 
 
 def solution(mesh):
+    meshes = mesh.shape["tensor"] == 1 and mesh.shape["expert"] == NZ * NY * NC
     return jax.shard_map(
-        local,
+        meshed if meshes else local,
         mesh=mesh,
         in_specs=(
             P(("group", "expert"), "tensor"),

time: 408 us -> 271 us (0.66)
  the two profiles are of different devices: /device:TPU:13 before, /device:TPU:0 now
where the time goes in v1:
time: 271 us; the launch traced here: 270 us
  Pallas kernels  190 us (70%)
  matrix products  69.1 us (25%)
  other arithmetic  7.66 us (3%)
    pallas_call x1, Pallas kernels, fold(): pl.pallas_call(functools.partial(fold_kernel, first), out_shape=jax.Shape...  95.4 us
    pallas_call x1, Pallas kernels, spread(): pl.pallas_call(functools.partial(spread_kernel, first), out_shape=jax.Sha...  94.7 us
    dot_general x2, matrix products, expert(): paired = jnp.einsum('nd,gdf->gnf', x, gate_up, preferred_element_type=F32)  27.8 us
    dot_general x2, matrix products, expert(): jnp.einsum('nf,fd->nd', hidden, down, preferred_element_type=F32)  18.6 us
    dot_general x1, matrix products, meshed(): part = jnp.einsum('brc,bcd->brd', hit, answers, preferred_element_type=F32)  12.4 us
    dot_general x1, matrix products, meshed(): jnp.einsum('brc,brd->bcd', hit, everything[:, :, :width], preferred_eleme...  10.2 us

profile of v1, /device:TPU:0, one launch (start us, length us, event | category | flops | bytes accessed | tf_op | source)
XLA Modules:
  0.0 270.2 jit_solution(16154976277301215017)
XLA Ops:
  0.0 0.7 reduce_sum.46
  0.7 0.7 select_reduce_fusion.2
  2.2 0.1 add_reduce_fusion
  2.3 0.1 iota_compare_fusion.3
  2.4 0.1 select_reduce_fusion.1
  2.5 0.1 copy.31
  2.7 2.2 fusion.33.x_ref
  4.9 94.7 %shard_map.82 = bf16[16,128,3712]{2,1,0:T(8,128)(2,1)} custom-call(bf16[128,3712]{1,0:T(8,128)(2,1)} %fusion.33.x_ref), custom_call_target="tpu_custom_call" | custom-call | tf_op jit(solution)/shard_map/pallas_call | solution.py:170
  99.5 1.3 select_reduce_fusion
  100.8 0.4 copy.32
  101.2 1.1 slice_convert_fusion
  102.3 0.9 fusion.32
  103.2 0.3 reduce_window_sum.18
  103.5 10.2 %fusion.6 = bf16[16,64,3584]{2,1,0:T(8,128)(2,1)} fusion(bf16[16,128,3712]{2,1,0:T(8,128)(2,1)} %shard_map.82, s32[16,128]{1,0:T(8,128)S(1)} %broadcast_add_fusion, pred[16,128]{1,0:T(8,128)(4,1)S(1)} %get-tuple-element.6), kind=kOutput, calls=%fused_computation.7 | convolution fusion | flops 943456256 | bytes 22030336 | tf_op jit(solution)/shard_map/brc,brd->bcd/dot_general | solution.py:385
  113.8 20.4 %fusion.22 = f32[2,1024,1024]{2,1,0:T(8,128)S(1)} fusion(bf16[1024,3584,1]{1,0,2:T(8,128)(2,1)} %bitcast.69, bf16[1,2,3584,1024]{3,2,1,0:T(8,128)(2,1)} %param.12), kind=kOutput, calls=%fused_computation.17 | convolution fusion | flops 15032385536 | bytes 30408704 | tf_op jit(solution)/shard_map/nd,gdf->gnf/dot_general | solution.py:397
  134.1 13.0 %convolution_convert_fusion = bf16[1024,3584]{1,0:T(8,128)(2,1)} fusion(bf16[1,1024,3584]{2,1,0:T(8,128)(2,1)} %param.13, f32[2,1024,1024]{2,1,0:T(8,128)S(1)} %fusion.22), kind=kOutput, calls=%fused_computation.8 | convolution fusion | flops 7526154240 | bytes 23068672 | tf_op jit(solution)/shard_map/nf,fd->nd/dot_general | solution.py:399
  147.1 0.0 copy-start
  147.1 12.4 %multiply_convert_fusion.p_ref = bf16[16,128,3584]{2,1,0:T(8,128)(2,1)} fusion(f32[16,128]{1,0:T(8,128)S(1)} %fusion.32, bf16[16,64,3584]{2,1,0:T(8,128)(2,1)} %bitcast.70, s32[16,128]{1,0:T(8,128)S(1)} %broadcast_add_fusion, pred[16,128]{1,0:T(8,128)(4,1)S(1)} %get-tuple-element.6), kind=kOutput, calls=%fused_computation | convolution fusion | flops 954466304 | bytes 22038528 | tf_op jit(solution)/shard_map/brc,bcd->brd/dot_general | solution.py:388
  159.6 0.0 copy-done
  159.6 7.4 %fusion.28 = f32[2,128,1024]{1,2,0:T(8,128)S(1)} fusion(bf16[1,2,3584,1024]{3,2,1,0:T(8,128)(2,1)} %param.14, bf16[128,3584]{1,0:T(8,128)(2,1)S(1)} %copy-done), kind=kOutput, calls=%fused_computation.21 | convolution fusion | flops 1879048192 | bytes 16646144 | tf_op jit(solution)/shard_map/nd,gdf->gnf/dot_general | solution.py:397
  167.0 5.6 %fusion.18.hot_ref = f32[128,3584]{1,0:T(8,128)} fusion(bf16[1,1024,3584]{2,1,0:T(8,128)(2,1)} %param.15, f32[128]{0:T(128)S(1)} %fusion.47, f32[2,128,1024]{1,2,0:T(8,128)S(1)} %fusion.28), kind=kOutput, calls=%fused_computation.14 | convolution fusion | flops 941686784 | bytes 10224128 | tf_op jit(solution)/shard_map/nf,fd->nd/dot_general | solution.py:399
  172.6 95.4 %shard_map.83 = bf16[128,3584]{1,0:T(8,128)(2,1)} custom-call(bf16[16,128,3584]{2,1,0:T(8,128)(2,1)} %multiply_convert_fusion.p_ref, f32[128,3584]{1,0:T(8,128)} %fusion.18.hot_ref), custom_call_target="tpu_custom_call" | custom-call | tf_op jit(solution)/shard_map/pallas_call | solution.py:333
  268.0 2.2 copy.37
  (10 shorter events, 0.1 us)
Async XLA Ops:
  147.1 12.4 %copy-start = (bf16[128,3584]{1,0:T(8,128)(2,1)S(1)}, bf16[128,3584]{1,0:T(8,128)(2,1)}, u32[]{:S(2)}) copy-start(bf16[128,3584]{1,0:T(8,128)(2,1)} %param.8) | copy-start | bytes 2752516

commit v2 on v1

--- a/solution.py
+++ b/solution.py
@@ -57,7 +57,9 @@
 def spread_kernel(first, x_ref, out_ref, own_sem, send_sem, recv_sem):
     z, y, c = place()
     rows = x_ref.shape[0]
-    parts = (pl.ds(0, first), pl.ds(first, rows - first))
+    half = first // 32 * 16
+    parts = (pl.ds(0, half), pl.ds(half, first - half), pl.ds(first, rows - first))
+    late = 2
     up, down, side, core = 0, 1, 2, 3
     own = index(z, y, c)
     keep = pltpu.make_async_copy(x_ref, out_ref.at[own], own_sem)
@@ -93,16 +95,16 @@
 
     has_up, has_down = z < NZ - 1, z > 0
     beside = index(z, 1 - y, c)
-    for part in (1, 0):
+    for part in (late, 0, 1):
         send(up, own, part, has_up, True)
         send(down, own, part, has_down, True)
         send(side, own, part, None, True)
-    for part in (0, 1):
+    for part in (0, 1, late):
         send(core, own, part, None, True)
-    arrived(beside, 1)
-    send(up, beside, 1, has_up)
-    send(down, beside, 1, has_down)
-    send(core, beside, 1)
+    arrived(beside, late)
+    send(up, beside, late, has_up)
+    send(down, beside, late, has_down)
+    send(core, beside, late)
 
     def step(k, finish):
         for way in (up, down):
@@ -113,7 +115,7 @@
             @pl.when(there)
             def _():
                 mine, other = index(zs, y, c), index(zs, 1 - y, c)
-                order = ((mine, 1), (mine, 0), (other, 1))
+                order = ((mine, late), (mine, 0), (mine, 1), (other, late))
                 for source, part in order:
                     if finish:
                         sent(way, source, part, onward)
@@ -121,11 +123,12 @@
                     else:
                         arrived(source, part)
                         send(way, source, part, onward)
-                        if part == 0:
+                        if part != late and source is mine:
                             send(side, source, part)
                         send(core, source, part)
                 if finish:
                     sent(side, mine, 0)
+                    sent(side, mine, 1)
 
     def cross(k, finish):
         for zs, there in ((z - k, z - k >= 0), (z + k, z + k < NZ)):
@@ -133,32 +136,34 @@
             @pl.when(there)
             def _():
                 other = index(zs, 1 - y, c)
-                if finish:
-                    sent(core, other, 0)
-                else:
-                    arrived(other, 0)
-                    send(core, other, 0)
+                for part in (0, 1):
+                    if finish:
+                        sent(core, other, part)
+                    else:
+                        arrived(other, part)
+                        send(core, other, part)
 
     for k in range(1, NZ):
         step(k, False)
         if k == 1:
-            arrived(beside, 0)
-            send(core, beside, 0)
+            for part in (0, 1):
+                arrived(beside, part)
+                send(core, beside, part)
         else:
             cross(k - 1, False)
     cross(NZ - 1, False)
     for zs in range(NZ):
         for ys in range(NY):
-            for part in (0, 1):
+            for part in (0, 1, late):
                 arrived(index(zs, ys, 1 - c), part)
-    for part in (1, 0):
+    for part in (0, 1, late):
         sent(up, own, part, has_up)
         sent(down, own, part, has_down)
         sent(side, own, part)
         sent(core, own, part)
         sent(core, beside, part)
-    sent(up, beside, 1, has_up)
-    sent(down, beside, 1, has_down)
+    sent(up, beside, late, has_up)
+    sent(down, beside, late, has_down)
     for k in range(1, NZ):
         step(k, True)
         cross(k, True)
@@ -174,15 +179,15 @@
         out_specs=pl.BlockSpec(memory_space=pl.ANY),
         scratch_shapes=[
             pltpu.SemaphoreType.DMA,
-            pltpu.SemaphoreType.DMA((4, n, 2)),
-            pltpu.SemaphoreType.DMA((n, 2)),
+            pltpu.SemaphoreType.DMA((4, n, 3)),
+            pltpu.SemaphoreType.DMA((n, 3)),
         ],
         compiler_params=pltpu.CompilerParams(collective_id=0, has_side_effects=True),
     )(x)
 
 
 def fold_kernel(
-    first, p_ref, hot_ref, o_ref, core_in, side_a, side_b, line_a, line_b, out_ya, out_yb, out_za, out_zb,
+    first, hid_ref, w_ref, hit_ref, share_ref, hot_ref, o_ref, p_ref, core_in, side_a, side_b, line_a, line_b, out_ya, out_yb, out_za, out_zb,
     core_s, core_r, ya_s, ya_r, yb_s, yb_r, za_s, za_r, zb_s, zb_r,
 ):
     z, y, c = place()
@@ -229,7 +234,21 @@
             pl.when(z + k < NZ)(lambda: f(z + k, 0))
             pl.when(z - k >= 0)(lambda: f(z - k, 1))
 
-    def start_core(zd, way):
+    def produce(zd, way):
+        width, tile = o_ref.shape[1], 512
+        cap = hit_ref.shape[2]
+
+        def one(t, carry):
+            cols = pl.ds(pl.multiple_of(t * tile, tile), tile)
+            answers = jnp.dot(hid_ref[zd], w_ref[:, cols], preferred_element_type=F32).astype(BF16)
+            for b in range(NY * NC):
+                mine = answers[b * cap : (b + 1) * cap]
+                at = zd * (NY * NC) + b
+                part = jnp.dot(hit_ref[at], mine, preferred_element_type=F32)
+                p_ref[at, :, cols] = (part * share_ref[at][:, :1]).astype(BF16)
+            return carry
+
+        lax.fori_loop(0, width // tile, one, 0)
         for yd in range(NY):
             core_copy(zd, yd).start()
 
@@ -312,11 +331,13 @@
             for yd in range(NY):
                 zb_copy(way, zd, yd).wait_send()
 
-    for k in (3, 2, 1, 0):
-        each(k, start_core)
+    each(3, produce)
+    each(2, produce)
     each(3, over_core)
+    each(1, produce)
     each(2, over_core)
     each(3, along)
+    each(0, produce)
     each(1, over_core)
     each(2, along)
     each(0, over_core)
@@ -326,16 +347,18 @@
         each(k, drain)
 
 
-def fold(parts, hot, first):
-    n, rows, width = parts.shape
+def fold(hidden, down, hit, share, hot, first):
+    n, rows = hit.shape[:2]
+    width = down.shape[1]
     rest = rows - first
     dma = pltpu.SemaphoreType.DMA
     return pl.pallas_call(
         functools.partial(fold_kernel, first),
         out_shape=jax.ShapeDtypeStruct((rows, width), BF16),
-        in_specs=[pl.BlockSpec(memory_space=pltpu.VMEM)] * 2,
+        in_specs=[pl.BlockSpec(memory_space=pltpu.VMEM)] * 5,
         out_specs=pl.BlockSpec(memory_space=pltpu.VMEM),
         scratch_shapes=[
+            pltpu.VMEM((n, rows, width), BF16),
             pltpu.VMEM((NZ, NY, rows, width), BF16),
             pltpu.VMEM((NZ, first, width), BF16),
             pltpu.VMEM((rest, width), BF16),
@@ -354,7 +377,7 @@
         compiler_params=pltpu.CompilerParams(
             collective_id=1, has_side_effects=True, vmem_limit_bytes=60 * 2**20
         ),
-    )(parts, hot)
+    )(hidden, down, hit, share, hot)
 
 
 def meshed(tokens, routes, gate_q, hot_list, cold_gate_up, cold_down, hot_gate_up, hot_down):
@@ -384,19 +407,21 @@
     hit = hit.astype(BF16)
     x = jnp.einsum("brc,brd->bcd", hit, everything[:, :, :width], preferred_element_type=F32)
     x = x.astype(BF16).reshape(n * capacity, width)
-    answers = expert(x, cold_gate_up[0], cold_down[0]).reshape(n, capacity, width)
-    part = jnp.einsum("brc,bcd->brd", hit, answers, preferred_element_type=F32)
-    part = (part * share[:, :, None]).astype(BF16)
+    hidden = hidden_of(x, cold_gate_up[0]).reshape(NZ, -1, cold_gate_up.shape[3])
+    share = jnp.broadcast_to(share[:, :, None], share.shape + (LANES,))
 
     hot_share = by_slot[:, n:].astype(F32) / whole.astype(F32)
     hot = hot_share * expert(tokens, hot_gate_up[0], hot_down[0]).astype(F32)
-    return fold(part, hot, first)
+    return fold(hidden, cold_down[0], hit, share, hot, first)
+
+
+def hidden_of(x, gate_up):
+    paired = jnp.einsum("nd,gdf->gnf", x, gate_up, preferred_element_type=F32)
+    return (jax.nn.silu(paired[0]) * paired[1]).astype(BF16)
 
 
 def expert(x, gate_up, down):
-    paired = jnp.einsum("nd,gdf->gnf", x, gate_up, preferred_element_type=F32)
-    hidden = (jax.nn.silu(paired[0]) * paired[1]).astype(BF16)
-    return jnp.einsum("nf,fd->nd", hidden, down, preferred_element_type=F32).astype(BF16)
+    return jnp.einsum("nf,fd->nd", hidden_of(x, gate_up), down, preferred_element_type=F32).astype(BF16)
 
 
 def slot_table(hot_list, experts_all):

time: 271 us -> 241 us (0.89)
  matrix products: 69.1 us -> 35.4 us
  other arithmetic: 7.66 us -> 12 us
    dot_general x5 -> x3, matrix products: 58.8 us -> 28.9 us  [the longest x2 26.4 us: hidden_of(): paired = jnp.einsum('nd,gdf->gnf', x, gate_up, preferred_element_type=F32)]
    pallas_call x1, Pallas kernels: 94.7 us -> 87.2 us  [spread(): pl.pallas_call(functools.partial(spread_kernel, first), out_shape=jax.Sha...]
    pallas_call x1, Pallas kernels: 95.4 us -> 101 us  [fold(): pl.pallas_call(functools.partial(fold_kernel, first), out_shape=jax.Shape...]
    convert_element_type x0 -> x2, other arithmetic: none -> 4.17 us  [the longest x1 2.78 us: hidden_of(): return (jax.nn.silu(paired[0]) * paired[1]).astype(BF16)]
    dot_general x1, matrix products: 10.2 us -> 6.52 us  [meshed(): jnp.einsum('brc,brd->bcd', hit, everything[:, :, :width], preferred_eleme...]
where the time goes in v2:
time: 241 us
  Pallas kernels  188 us (78%)
  matrix products  35.4 us (15%)
  other arithmetic  12 us (5%)
  local copies, waits for them, and re-layouts  4.83 us (2%)
    pallas_call x1, Pallas kernels, fold(): pl.pallas_call(functools.partial(fold_kernel, first), out_shape=jax.Shape...  101 us
    pallas_call x1, Pallas kernels, spread(): pl.pallas_call(functools.partial(spread_kernel, first), out_shape=jax.Sha...  87.2 us
    dot_general x2, matrix products, hidden_of(): paired = jnp.einsum('nd,gdf->gnf', x, gate_up, preferred_element_type=F32)  26.4 us
    dot_general x1, matrix products, meshed(): jnp.einsum('brc,brd->bcd', hit, everything[:, :, :width], preferred_eleme...  6.52 us

profile of v2, /device:TPU:0, one launch (start us, length us, event | category | flops | bytes accessed | tf_op | source)
XLA Modules:
  0.0 241.0 jit_solution(4146262550816521095)
XLA Ops:
  0.7 0.7 reduce_sum.46
  1.4 0.7 select_reduce_fusion.2
  2.2 0.1 add_reduce_fusion
  2.3 0.1 iota_compare_fusion.3
  2.4 0.1 select_reduce_fusion.1
  2.5 0.1 copy.34
  2.7 0.0 slice-start
  2.7 2.3 fusion.32.x_ref
  5.0 0.0 slice-start.1
  5.0 7.7 %fusion.24 = f32[2,128,1024]{1,2,0:T(8,128)S(1)} fusion(bf16[1,2,3584,1024]{3,2,1,0:T(8,128)(2,1)} %param.14, bf16[128,3584]{1,0:T(8,128)(2,1)} %param.8), kind=kOutput, calls=%fused_computation.16 | convolution fusion | flops 1879048192 | bytes 16646144 | tf_op jit(solution)/shard_map/nd,gdf->gnf/dot_general | solution.py:419
  12.7 0.0 slice-done
  12.8 0.0 slice-done.1
  12.8 2.5 %fusion.17.hot_ref = f32[128,3584]{1,0:T(8,128)} fusion(bf16[1,1024,3584]{2,1,0:T(8,128)(2,1)S(1)} %bitcast.65, f32[128]{0:T(128)S(1)} %fusion.41, f32[2,128,1024]{1,2,0:T(8,128)S(1)} %fusion.24), kind=kOutput, calls=%fused_computation.11 | convolution fusion | flops 941686784 | bytes 10224128 | tf_op jit(solution)/shard_map/nf,fd->nd/dot_general | solution.py:424
  15.2 87.2 %shard_map.82 = bf16[16,128,3712]{2,1,0:T(8,128)(2,1)} custom-call(bf16[128,3712]{1,0:T(8,128)(2,1)} %fusion.32.x_ref), custom_call_target="tpu_custom_call" | custom-call | tf_op jit(solution)/shard_map/pallas_call | solution.py:175
  102.4 1.3 select_reduce_fusion
  103.7 0.3 reduce_window_sum.18
  104.0 1.4 fusion.30.hit_ref
  105.4 0.4 copy.36
  105.8 1.1 slice_convert_fusion
  106.9 6.5 %fusion.6 = bf16[16,64,3584]{2,1,0:T(8,128)(2,1)S(1)} fusion(bf16[16,128,3712]{2,1,0:T(8,128)(2,1)} %shard_map.82, s32[16,128]{1,0:T(8,128)S(1)} %broadcast_add_fusion, pred[16,128]{1,0:T(8,128)(4,1)S(1)} %get-tuple-element.6), kind=kOutput, calls=%fused_computation.6 | convolution fusion | flops 943456256 | bytes 22030336 | tf_op jit(solution)/shard_map/brc,brd->bcd/dot_general | solution.py:408
  113.4 0.9 fusion.28
  114.3 1.3 broadcast_in_dim.74.share_ref
  115.7 18.7 %fusion.20 = f32[2,1024,1024]{2,1,0:T(8,128)S(1)} fusion(bf16[1024,3584,1]{1,0,2:T(8,128)(2,1)S(1)} %bitcast.68, bf16[1,2,3584,1024]{3,2,1,0:T(8,128)(2,1)} %param.12), kind=kOutput, calls=%fused_computation.13 | convolution fusion | flops 15032385536 | bytes 30408704 | tf_op jit(solution)/shard_map/nd,gdf->gnf/dot_general | solution.py:419
  134.3 0.8 fusion.45
  135.2 2.8 %multiply_convert_fusion.hid_ref = bf16[4,256,1024]{2,1,0:T(8,128)(2,1)} fusion(f32[4,256,1024]{2,1,0:T(8,128)S(1)} %bitcast.67, f32[4,256,1024]{2,1,0:T(8,128)S(1)} %bitcast.66), kind=kLoop, calls=%fused_computation.12 | loop fusion | flops 6291456 | bytes 10485760 | tf_op jit(solution)/shard_map/convert_element_type | solution.py:420
  138.0 100.8 %shard_map.83 = bf16[128,3584]{1,0:T(8,128)(2,1)} custom-call(bf16[4,256,1024]{2,1,0:T(8,128)(2,1)} %multiply_convert_fusion.hid_ref, bf16[1024,3584]{1,0:T(8,128)(2,1)} %bitcast.69, bf16[16,128,64]{2,1,0:T(8,128)(2,1)} %fusion.30.hit_ref, f32[16,128,128]{2,1,0:T(8,128)} %broadcast_in_dim.74.share_ref, f32[128,3584]{1,0:T(8,128)} %fusion.17.hot_ref), custom_call_target="tpu_custom_call" | custom-call | tf_op jit(solution)/shard_map/pallas_call | solution.py:355
  238.8 2.2 copy.42
  (11 shorter events, 0.1 us)
Async XLA Ops:
  2.7 10.1 %slice-start = ((s8[7340032]{0:T(1024)(128)(4,1)}), s8[4194304]{0:T(1024)(128)(4,1)S(1)}, s32[]{:S(2)}) async-start(s8[7340032]{0:T(1024)(128)(4,1)} %bitcast.64), calls=%async_computation | async-start | bytes 8388608
  5.0 7.7 %slice-start.1 = ((s8[7340032]{0:T(1024)(128)(4,1)}), s8[3145728]{0:T(1024)(128)(4,1)S(1)}, s32[]{:S(2)}) async-start(s8[7340032]{0:T(1024)(128)(4,1)} %bitcast.64), calls=%async_computation.1 | async-start | bytes 6291456

commit v3 on v2

--- a/solution.py
+++ b/solution.py
@@ -54,7 +54,9 @@
         pl.semaphore_wait(barrier, 4)
 
 
-def spread_kernel(first, x_ref, out_ref, own_sem, send_sem, recv_sem):
+def spread_kernel(
+    first, x_ref, gu_ref, dn_ref, out_ref, hot_ref, x_in, gu_in, dn_in, mid, own_sem, load_sem, send_sem, recv_sem
+):
     z, y, c = place()
     rows = x_ref.shape[0]
     half = first // 32 * 16
@@ -64,6 +66,12 @@
     own = index(z, y, c)
     keep = pltpu.make_async_copy(x_ref, out_ref.at[own], own_sem)
     keep.start()
+    loads = [
+        pltpu.make_async_copy(src, dst, load_sem.at[i])
+        for i, (src, dst) in enumerate(((x_ref, x_in), (gu_ref, gu_in), (dn_ref, dn_in)))
+    ]
+    for load in loads:
+        load.start()
     greet(z, y, c)
 
     def copy(way, source, part, from_input=False):
@@ -143,9 +151,31 @@
                         arrived(other, part)
                         send(core, other, part)
 
+    def hot_expert():
+        for load in loads:
+            load.wait()
+        tile, depth = 256, gu_in.shape[1]
+
+        def paired(t, carry):
+            cols = pl.ds(pl.multiple_of(t * tile, tile), tile)
+            gate = jnp.dot(x_in[:, :depth], gu_in[0, :, cols], preferred_element_type=F32)
+            up_ = jnp.dot(x_in[:, :depth], gu_in[1, :, cols], preferred_element_type=F32)
+            mid[:, cols] = (jax.nn.silu(gate) * up_).astype(BF16)
+            return carry
+
+        lax.fori_loop(0, gu_in.shape[2] // tile, paired, 0)
+
+        def answer(t, carry):
+            cols = pl.ds(pl.multiple_of(t * tile, tile), tile)
+            hot_ref[:, cols] = jnp.dot(mid[...], dn_in[:, cols], preferred_element_type=F32).astype(BF16)
+            return carry
+
+        lax.fori_loop(0, depth // tile, answer, 0)
+
     for k in range(1, NZ):
         step(k, False)
         if k == 1:
+            hot_expert()
             for part in (0, 1):
                 arrived(beside, part)
                 send(core, beside, part)
@@ -170,20 +200,30 @@
     keep.wait()
 
 
-def spread(x, first):
+def spread(x, gate_up, down, first):
     n = NZ * NY * NC
     return pl.pallas_call(
         functools.partial(spread_kernel, first),
-        out_shape=jax.ShapeDtypeStruct((n,) + x.shape, x.dtype),
-        in_specs=[pl.BlockSpec(memory_space=pl.ANY)],
-        out_specs=pl.BlockSpec(memory_space=pl.ANY),
+        out_shape=[
+            jax.ShapeDtypeStruct((n,) + x.shape, x.dtype),
+            jax.ShapeDtypeStruct((x.shape[0], down.shape[1]), BF16),
+        ],
+        in_specs=[pl.BlockSpec(memory_space=pl.ANY)] * 3,
+        out_specs=[pl.BlockSpec(memory_space=pl.ANY), pl.BlockSpec(memory_space=pltpu.VMEM)],
         scratch_shapes=[
+            pltpu.VMEM(x.shape, BF16),
+            pltpu.VMEM(gate_up.shape, BF16),
+            pltpu.VMEM(down.shape, BF16),
+            pltpu.VMEM((x.shape[0], down.shape[0]), BF16),
             pltpu.SemaphoreType.DMA,
+            pltpu.SemaphoreType.DMA((3,)),
             pltpu.SemaphoreType.DMA((4, n, 3)),
             pltpu.SemaphoreType.DMA((n, 3)),
         ],
-        compiler_params=pltpu.CompilerParams(collective_id=0, has_side_effects=True),
-    )(x)
+        compiler_params=pltpu.CompilerParams(
+            collective_id=0, has_side_effects=True, vmem_limit_bytes=48 * 2**20
+        ),
+    )(x, gate_up, down)
 
 
 def fold_kernel(
@@ -394,7 +434,9 @@
     whole = jnp.sum(gate_q, axis=1, keepdims=True)
     extra = jnp.concatenate([by_slot[:, :n], whole // 256, whole % 256], axis=1).astype(BF16)
     extra = jnp.pad(extra, ((0, 0), (0, LANES - extra.shape[1])))
-    everything = spread(jnp.concatenate([tokens, extra], axis=1), first)
+    everything, hot_answer = spread(
+        jnp.concatenate([tokens, extra], axis=1), hot_gate_up[0], hot_down[0], first
+    )
 
     notes = everything[:, :, width:].astype(F32)
     slot = lax.axis_index("expert")
@@ -411,17 +453,13 @@
     share = jnp.broadcast_to(share[:, :, None], share.shape + (LANES,))
 
     hot_share = by_slot[:, n:].astype(F32) / whole.astype(F32)
-    hot = hot_share * expert(tokens, hot_gate_up[0], hot_down[0]).astype(F32)
+    hot = hot_share * hot_answer.astype(F32)
     return fold(hidden, cold_down[0], hit, share, hot, first)
 
 
 def hidden_of(x, gate_up):
     paired = jnp.einsum("nd,gdf->gnf", x, gate_up, preferred_element_type=F32)
     return (jax.nn.silu(paired[0]) * paired[1]).astype(BF16)
-
-
-def expert(x, gate_up, down):
-    return jnp.einsum("nf,fd->nd", hidden_of(x, gate_up), down, preferred_element_type=F32).astype(BF16)
 
 
 def slot_table(hot_list, experts_all):

time: 241 us -> 232 us (0.963)
  matrix products: 35.4 us -> 25.2 us
    dot_general x2 -> x1, matrix products: 26.4 us -> 18.7 us  [hidden_of(): paired = jnp.einsum('nd,gdf->gnf', x, gate_up, preferred_element_type=F32)]
    dot_general x1 -> x0, matrix products: 2.46 us -> none  [expert(): jnp.einsum('nf,fd->nd', hidden_of(x, gate_up), down, preferred_element_ty...]
where the time goes in v3:
time: 232 us; the launch traced here: 231 us
  Pallas kernels  188 us (81%)
  matrix products  25.2 us (11%)
  other arithmetic  12.3 us (5%)
  local copies, waits for them, and re-layouts  4.82 us (2%)
    pallas_call x1, Pallas kernels, fold(): pl.pallas_call(functools.partial(fold_kernel, first), out_shape=jax.Shape...  101 us
    pallas_call x1, Pallas kernels, spread(): pl.pallas_call(functools.partial(spread_kernel, first), out_shape=[jax.Sh...  87.4 us
    dot_general x1, matrix products, hidden_of(): paired = jnp.einsum('nd,gdf->gnf', x, gate_up, preferred_element_type=F32)  18.7 us
    dot_general x1, matrix products, meshed(): jnp.einsum('brc,brd->bcd', hit, everything[:, :, :width], preferred_eleme...  6.52 us

profile of v3, /device:TPU:0, one launch (start us, length us, event | category | flops | bytes accessed | tf_op | source)
XLA Modules:
  0.0 231.3 jit_solution(12489237892471135214)
XLA Ops:
  0.7 0.7 reduce_sum.46
  1.4 0.7 select_reduce_fusion.2
  2.2 0.1 add_reduce_fusion
  2.3 0.1 iota_compare_fusion.3
  2.4 0.1 select_reduce_fusion.1
  2.5 0.1 copy.31
  2.7 1.2 fusion.16.x_ref
  3.9 87.4 %shard_map.82 = (bf16[16,128,3712]{2,1,0:T(8,128)(2,1)}, bf16[128,3584]{1,0:T(8,128)(2,1)S(1)}) custom-call(bf16[128,3712]{1,0:T(8,128)(2,1)S(1)} %fusion.16.x_ref, bf16[2,3584,1024]{2,1,0:T(8,128)(2,1)} %bitcast.47, bf16[1024,3584]{1,0:T(8,128)(2,1)} %bitcast.48), custom_call_target="tpu_custom_call" | custom-call | tf_op jit(solution)/shard_map/pallas_call | solution.py:205
  91.3 1.3 select_reduce_fusion
  92.6 0.3 reduce_window_sum.18
  92.9 1.4 fusion.14.hit_ref
  94.3 1.4 convert_multiply_fusion.hot_ref
  95.7 0.4 copy.33
  96.1 1.1 slice_convert_fusion
  97.2 6.5 %fusion.4 = bf16[16,64,3584]{2,1,0:T(8,128)(2,1)S(1)} fusion(bf16[16,128,3712]{2,1,0:T(8,128)(2,1)} %get-tuple-element.7, s32[16,128]{1,0:T(8,128)S(1)} %broadcast_add_fusion, pred[16,128]{1,0:T(8,128)(4,1)S(1)} %get-tuple-element.10), kind=kOutput, calls=%fused_computation.4 | convolution fusion | flops 943456256 | bytes 22030336 | tf_op jit(solution)/shard_map/brc,brd->bcd/dot_general | solution.py:450
  103.8 0.9 fusion.12
  104.7 1.3 broadcast_in_dim.74.share_ref
  106.0 18.7 %fusion.7 = f32[2,1024,1024]{2,1,0:T(8,128)S(1)} fusion(bf16[1024,3584,1]{1,0,2:T(8,128)(2,1)S(1)} %bitcast.46, bf16[1,2,3584,1024]{3,2,1,0:T(8,128)(2,1)} %param.12), kind=kOutput, calls=%fused_computation.6 | convolution fusion | flops 15032385536 | bytes 30408704 | tf_op jit(solution)/shard_map/nd,gdf->gnf/dot_general | solution.py:461
  124.7 0.8 fusion.24
  125.5 2.8 %multiply_convert_fusion.hid_ref = bf16[4,256,1024]{2,1,0:T(8,128)(2,1)} fusion(f32[4,256,1024]{2,1,0:T(8,128)S(1)} %bitcast.45, f32[4,256,1024]{2,1,0:T(8,128)S(1)} %bitcast.44), kind=kLoop, calls=%fused_computation.5 | loop fusion | flops 6291456 | bytes 10485760 | tf_op jit(solution)/shard_map/convert_element_type | solution.py:462
  128.3 100.8 %shard_map.83 = bf16[128,3584]{1,0:T(8,128)(2,1)} custom-call(bf16[4,256,1024]{2,1,0:T(8,128)(2,1)} %multiply_convert_fusion.hid_ref, bf16[1024,3584]{1,0:T(8,128)(2,1)} %bitcast.49, bf16[16,128,64]{2,1,0:T(8,128)(2,1)} %fusion.14.hit_ref, f32[16,128,128]{2,1,0:T(8,128)} %broadcast_in_dim.74.share_ref, f32[128,3584]{1,0:T(8,128)} %convert_multiply_fusion.hot_ref), custom_call_target="tpu_custom_call" | custom-call | tf_op jit(solution)/shard_map/pallas_call | solution.py:395
  229.1 2.2 copy.37
  (10 shorter events, 0.1 us)
